TPU v7x, 128 devices: a whole 4x4x4 slice. The times are simulated.
128 devices in a mesh: space: 32 (over x, z, core), col: 4 (over y).
Axes of the slice: x: 4, y: 4, z: 4, core: 2. Of those that a mesh axis runs over, the one named last changes fastest.
Arguments:
- test_matrix: bfloat16 [256, 3712], P('col'), may hold values from -6 to 6
- anomalies: bfloat16 [3712, 65536], P(None, 'space'), may hold values from -32 to 32
Outputs:
- eofs: float32 [256, 65536], P('col', 'space')
- pcs: float32 [256, 3712], P('col')
All inputs are finite; a program needn't handle non-finite values.
Results may differ from a plain program's by a relative error of at most 0.03.
Values may be sent and summed in bfloat16 or wider, within the bound.
A program may use at most 64 MiB of HBM per device.

v0:
```python
import jax
import jax.numpy as jnp
from jax import lax
from jax.sharding import PartitionSpec as P

ITERS = 2


def contract_rows(first, second):
    return lax.dot_general(
        first, second, (((1,), (1,)), ((), ())), preferred_element_type=jnp.float32
    )


def body(test_matrix, anomalies):
    col_width = test_matrix.shape[0]
    col_index = lax.axis_index("col")
    grid_total = anomalies.shape[1] * lax.axis_size("space")
    full_width = col_width * lax.axis_size("col")

    def widen_basis(left_factor):
        whole_basis = jnp.dot(
            lax.all_gather(left_factor, "col", axis=0, tiled=True),
            anomalies,
            preferred_element_type=jnp.float32,
        ).astype(jnp.bfloat16)
        own_rows = lax.dynamic_slice_in_dim(whole_basis, col_index * col_width, col_width, 0)
        return (whole_basis, own_rows)

    def orthonormalize(whole_basis):
        gram_sum = lax.psum(
            contract_rows(whole_basis, whole_basis).astype(jnp.bfloat16), "space"
        ).astype(jnp.float32)
        lower_factor = jnp.linalg.cholesky(gram_sum / grid_total)
        identity_matrix = jnp.eye(full_width, dtype=jnp.float32)
        inverse = jax.scipy.linalg.solve_triangular(
            lower_factor, identity_matrix, lower=True
        ).astype(jnp.bfloat16)
        own_inverse = lax.dynamic_slice_in_dim(inverse, col_index * col_width, col_width, 0)
        return jnp.dot(own_inverse, whole_basis, preferred_element_type=jnp.float32)

    def project_scores(orthonormal):
        partial_sum = contract_rows(orthonormal.astype(jnp.bfloat16), anomalies)
        return lax.psum(partial_sum.astype(jnp.bfloat16), "space").astype(jnp.float32) / grid_total

    whole_basis, own_rows = widen_basis(test_matrix)
    orthonormal = orthonormalize(whole_basis)
    projected = project_scores(orthonormal)
    for iteration in range(ITERS):
        whole_basis, own_rows = widen_basis(projected.astype(jnp.bfloat16))
        orthonormal = orthonormalize(whole_basis)
        projected = project_scores(orthonormal)
    return (orthonormal, projected)


def solution(mesh):
    return jax.shard_map(
        body,
        mesh=mesh,
        in_specs=(P("col", None), P(None, "space")),
        out_specs=(P("col", "space"), P("col", None)),
        check_vma=False,
    )
```

profile of v0, /device:TPU:1, one launch (start us, length us, event | category | flops | bytes accessed | tf_op | source)
XLA Modules:
  0.0 975.7 jit_solution(3879057552766252499)
XLA Ops:
  7.2 0.7 all-gather.4.cloned.1.call-update
  8.0 34.2 %all-gather.4.cloned.1.call-done = bf16[256,3712]{1,0:T(8,128)(2,1)} async-done(((bf16[64,3712]{1,0:T(8,128)(2,1)}), bf16[256,3712]{1,0:T(8,128)(2,1)}) %all-gather.4.cloned.1.call-update) | async-done | bytes 1900560 | tf_op jit(solution)/shard_map/all_gather | solution.py:23
  42.1 10.1 %convolution_convert_fusion.5 = bf16[256,2048]{1,0:T(8,128)(2,1)S(1)} fusion(bf16[256,3712]{1,0:T(8,128)(2,1)} %all-gather.4.cloned.1.call-done, bf16[3712,2048]{1,0:T(8,128)(2,1)} %param.6), kind=kOutput, calls=%fused_computation.11 | convolution fusion | flops 3892838400 | bytes 18153472 | tf_op jit(solution)/shard_map/dot_general | solution.py:22
  52.3 1.1 convolution_convert_fusion.10
  53.7 99.6 %all-reduce.8.cloned.1.call-done = bf16[256,256]{0,1:T(8,128)(2,1)} async-done(((bf16[256,256]{0,1:T(8,128)(2,1)}), bf16[256,256]{0,1:T(8,128)(2,1)}) %all-reduce.8.cloned.1.call-update) | async-done | bytes 131088 | tf_op jit(solution)/shard_map/psum | solution.py:31
  153.3 0.9 convert_multiply_fusion.3
  154.4 0.9 fusion.2
  155.3 11.7 %cholesky.172 = f32[128,128]{1,0:T(8,128)S(1)} custom-call(f32[128,128]{1,0:T(8,128)S(1)} %cholesky.270), custom_call_target="Cholesky" | custom-call | tf_op jit(solution)/shard_map/jit(cholesky)/cholesky | solution.py:34
  167.1 9.8 %custom-call.15 = f32[1,128,128]{1,2,0:T(8,128)S(1)} custom-call(f32[1,128,128]{2,1,0:T(8,128)S(1)} %get-tuple-element.68), custom_call_target="InvertDiagBlocksLowerTriangular" | custom-call | tf_op jit(solution)/shard_map/jit(cholesky)/cholesky | solution.py:34
  177.4 11.7 %cholesky.189 = f32[128,128]{1,0:T(8,128)S(1)} custom-call(f32[128,128]{1,0:T(8,128)S(1)} %convolution_subtract_fusion.5), custom_call_target="Cholesky" | custom-call | tf_op jit(solution)/shard_map/jit(cholesky)/cholesky | solution.py:34
  189.1 0.7 compare_reduce_fusion.4
  191.3 4.3 while.6
  191.6 0.6 fusion.92
  192.2 1.4 bitcast_dynamic-update-slice_fusion.6
  193.6 0.6 fusion.92
  194.2 1.4 bitcast_dynamic-update-slice_fusion.6
  195.7 19.7 %custom-call.16 = f32[2,128,128]{1,2,0:T(8,128)S(1)} custom-call(f32[2,128,128]{2,1,0:T(8,128)S(1)} %get-tuple-element.24), custom_call_target="InvertDiagBlocksLowerTriangular" | custom-call | tf_op jit(solution)/shard_map/jit(_solve_triangular)/triangular_solve | solution.py:36
  215.9 0.3 fusion.26
  216.3 9.0 convolution_convert_fusion.2
  225.3 103.1 %all-reduce.10.cloned.1.call-done = bf16[64,3712]{1,0:T(8,128)(2,1)} async-done(((bf16[64,3712]{1,0:T(8,128)(2,1)}), bf16[64,3712]{1,0:T(8,128)(2,1)}) %all-reduce.10.cloned.1.call-update) | async-done | bytes 475152 | tf_op jit(solution)/shard_map/psum | solution.py:44
  328.4 1.9 multiply_convert_fusion.1
  330.4 29.2 %all-gather.6.cloned.1.call-done = bf16[256,3712]{1,0:T(8,128)(2,1)} async-done(((bf16[64,3712]{1,0:T(8,128)(2,1)}), bf16[256,3712]{1,0:T(8,128)(2,1)}) %all-gather.6.cloned.1.call-update) | async-done | bytes 1900560 | tf_op jit(solution)/shard_map/all_gather | solution.py:23
  359.6 10.1 %convolution_convert_fusion.4 = bf16[256,2048]{1,0:T(8,128)(2,1)S(1)} fusion(bf16[256,3712]{1,0:T(8,128)(2,1)} %all-gather.6.cloned.1.call-done, bf16[3712,2048]{1,0:T(8,128)(2,1)} %param.6), kind=kOutput, calls=%fused_computation.10 | convolution fusion | flops 3892838400 | bytes 18153472 | tf_op jit(solution)/shard_map/dot_general | solution.py:22
  369.7 1.1 convolution_convert_fusion.9
  370.9 0.4 all-reduce.14.cloned.1.call-start
  371.3 99.5 %all-reduce.12.cloned.1.call-done = bf16[256,256]{0,1:T(8,128)(2,1)} async-done(((bf16[256,256]{0,1:T(8,128)(2,1)}), bf16[256,256]{0,1:T(8,128)(2,1)}) %all-reduce.12.cloned.1.call-update) | async-done | bytes 131088 | tf_op jit(solution)/shard_map/psum | solution.py:31
  470.8 0.9 convert_multiply_fusion.2
  471.9 0.9 fusion.1
  472.8 11.7 %cholesky.206 = f32[128,128]{1,0:T(8,128)S(1)} custom-call(f32[128,128]{1,0:T(8,128)S(1)} %cholesky.273), custom_call_target="Cholesky" | custom-call | tf_op jit(solution)/shard_map/jit(cholesky)/cholesky | solution.py:34
  484.6 9.8 %custom-call.17 = f32[1,128,128]{1,2,0:T(8,128)S(1)} custom-call(f32[1,128,128]{2,1,0:T(8,128)S(1)} %get-tuple-element.64), custom_call_target="InvertDiagBlocksLowerTriangular" | custom-call | tf_op jit(solution)/shard_map/jit(cholesky)/cholesky | solution.py:34
  494.9 11.7 %cholesky.223 = f32[128,128]{1,0:T(8,128)S(1)} custom-call(f32[128,128]{1,0:T(8,128)S(1)} %convolution_subtract_fusion.4), custom_call_target="Cholesky" | custom-call | tf_op jit(solution)/shard_map/jit(cholesky)/cholesky | solution.py:34
  506.6 0.7 compare_reduce_fusion.2
  507.4 0.6 compare_reduce_fusion.3
  509.4 4.3 while.7
  509.6 0.6 fusion.93
  510.2 1.4 bitcast_dynamic-update-slice_fusion.7
  511.6 0.6 fusion.93
  512.2 1.4 bitcast_dynamic-update-slice_fusion.7
  513.7 19.7 %custom-call.18 = f32[2,128,128]{1,2,0:T(8,128)S(1)} custom-call(f32[2,128,128]{2,1,0:T(8,128)S(1)} %get-tuple-element.25), custom_call_target="InvertDiagBlocksLowerTriangular" | custom-call | tf_op jit(solution)/shard_map/jit(_solve_triangular)/triangular_solve | solution.py:36
  533.9 0.3 fusion.22
  534.3 9.0 convolution_convert_fusion.1
  543.3 103.1 %all-reduce.14.cloned.1.call-done = bf16[64,3712]{1,0:T(8,128)(2,1)} async-done(((bf16[64,3712]{1,0:T(8,128)(2,1)}), bf16[64,3712]{1,0:T(8,128)(2,1)}) %all-reduce.14.cloned.1.call-update) | async-done | bytes 475152 | tf_op jit(solution)/shard_map/psum | solution.py:44
  646.4 1.9 multiply_convert_fusion
  648.3 29.4 %all-gather.8.cloned.1.call-done = bf16[256,3712]{1,0:T(8,128)(2,1)} async-done(((bf16[64,3712]{1,0:T(8,128)(2,1)}), bf16[256,3712]{1,0:T(8,128)(2,1)}) %all-gather.8.cloned.1.call-update) | async-done | bytes 1900560 | tf_op jit(solution)/shard_map/all_gather | solution.py:23
  677.7 10.1 %convolution_convert_fusion.3 = bf16[256,2048]{1,0:T(8,128)(2,1)S(1)} fusion(bf16[256,3712]{1,0:T(8,128)(2,1)} %all-gather.8.cloned.1.call-done, bf16[3712,2048]{1,0:T(8,128)(2,1)} %param.6), kind=kOutput, calls=%fused_computation.9 | convolution fusion | flops 3892838400 | bytes 18153472 | tf_op jit(solution)/shard_map/dot_general | solution.py:22
  687.8 1.1 convolution_convert_fusion.8
  689.3 99.6 %all-reduce.16.cloned.1.call-done = bf16[256,256]{0,1:T(8,128)(2,1)} async-done(((bf16[256,256]{0,1:T(8,128)(2,1)}), bf16[256,256]{0,1:T(8,128)(2,1)}) %all-reduce.16.cloned.1.call-update) | async-done | bytes 131088 | tf_op jit(solution)/shard_map/psum | solution.py:31
  788.9 0.9 convert_multiply_fusion.1
  789.9 0.9 fusion
  790.9 11.7 %cholesky.240 = f32[128,128]{1,0:T(8,128)S(1)} custom-call(f32[128,128]{1,0:T(8,128)S(1)} %cholesky.276), custom_call_target="Cholesky" | custom-call | tf_op jit(solution)/shard_map/jit(cholesky)/cholesky | solution.py:34
  802.7 9.8 %custom-call.19 = f32[1,128,128]{1,2,0:T(8,128)S(1)} custom-call(f32[1,128,128]{2,1,0:T(8,128)S(1)} %get-tuple-element.60), custom_call_target="InvertDiagBlocksLowerTriangular" | custom-call | tf_op jit(solution)/shard_map/jit(cholesky)/cholesky | solution.py:34
  813.0 11.7 %cholesky.257 = f32[128,128]{1,0:T(8,128)S(1)} custom-call(f32[128,128]{1,0:T(8,128)S(1)} %convolution_subtract_fusion.3), custom_call_target="Cholesky" | custom-call | tf_op jit(solution)/shard_map/jit(cholesky)/cholesky | solution.py:34
  824.7 0.7 compare_reduce_fusion
  825.4 0.6 compare_reduce_fusion.1
  827.5 4.4 while.8
  827.7 0.6 fusion.94
  828.3 1.4 bitcast_dynamic-update-slice_fusion.8
  829.8 0.6 fusion.94
  830.4 1.4 bitcast_dynamic-update-slice_fusion.8
  831.8 19.7 %custom-call.20 = f32[2,128,128]{1,2,0:T(8,128)S(1)} custom-call(f32[2,128,128]{2,1,0:T(8,128)S(1)} %get-tuple-element.26), custom_call_target="InvertDiagBlocksLowerTriangular" | custom-call | tf_op jit(solution)/shard_map/jit(_solve_triangular)/triangular_solve | solution.py:36
  852.1 0.3 fusion.18
  852.7 11.0 %convolution_convert_fusion = bf16[64,3712]{1,0:T(8,128)(2,1)} fusion(bf16[3712,2048]{1,0:T(8,128)(2,1)} %param.6, f32[64,2048]{1,0:T(8,128)S(1)} %fusion.44), kind=kOutput, calls=%fused_computation.6 | convolution fusion | flops 973447168 | bytes 16203776 | tf_op jit(solution)/shard_map/dot_general | solution.py:10
  863.7 103.1 %all-reduce.18.cloned.1.call-done = bf16[64,3712]{1,0:T(8,128)(2,1)} async-done(((bf16[64,3712]{1,0:T(8,128)(2,1)}), bf16[64,3712]{1,0:T(8,128)(2,1)}) %all-reduce.18.cloned.1.call-update) | async-done | bytes 475152 | tf_op jit(solution)/shard_map/psum | solution.py:44
  966.9 2.0 convert_multiply_fusion
  (61 shorter events, 5.2 us)
Async XLA Ops:
  7.2 35.0 %all-gather.4.cloned.1.call-start = ((), (), s32[]{:S(2)}) async-start(), calls=%async_computation | async-start | bytes 2375680 | tf_op jit(solution)/shard_map/all_gather | solution.py:23
  7.9 145.4 %all-reduce.8.cloned.1.call-start = ((), (), s32[]{:S(2)}) async-start(), calls=%async_computation.1 | async-start | bytes 262144 | tf_op jit(solution)/shard_map/psum | solution.py:31
  53.4 275.0 %all-reduce.10.cloned.1.call-start = ((), (), s32[]{:S(2)}) async-start(), calls=%async_computation.2 | async-start | bytes 950272 | tf_op jit(solution)/shard_map/psum | solution.py:44
  225.3 134.3 %all-gather.6.cloned.1.call-start = ((), (), s32[]{:S(2)}) async-start(), calls=%async_computation.3 | async-start | bytes 2375680 | tf_op jit(solution)/shard_map/all_gather | solution.py:23
  330.3 140.5 %all-reduce.12.cloned.1.call-start = ((), (), s32[]{:S(2)}) async-start(), calls=%async_computation.4 | async-start | bytes 262144 | tf_op jit(solution)/shard_map/psum | solution.py:31
  370.9 275.5 %all-reduce.14.cloned.1.call-start = ((), (), s32[]{:S(2)}) async-start(), calls=%async_computation.5 | async-start | bytes 950272 | tf_op jit(solution)/shard_map/psum | solution.py:44
  543.3 134.4 %all-gather.8.cloned.1.call-start = ((), (), s32[]{:S(2)}) async-start(), calls=%async_computation.6 | async-start | bytes 2375680 | tf_op jit(solution)/shard_map/all_gather | solution.py:23
  648.3 140.6 %all-reduce.16.cloned.1.call-start = ((), (), s32[]{:S(2)}) async-start(), calls=%async_computation.7 | async-start | bytes 262144 | tf_op jit(solution)/shard_map/psum | solution.py:31
  689.0 277.9 %all-reduce.18.cloned.1.call-start = ((), (), s32[]{:S(2)}) async-start(), calls=%async_computation.8 | async-start | bytes 950272 | tf_op jit(solution)/shard_map/psum | solution.py:44
  852.7 116.2 %copy-start = (f32[64,2048]{1,0:T(8,128)}, f32[64,2048]{1,0:T(8,128)S(1)}, u32[]{:S(2)}) copy-start(f32[64,2048]{1,0:T(8,128)S(1)} %fusion.44) | copy-start | bytes 1572868
Sparse Core Ops, SparseCore 0:
  9.7 32.4 all-gather.3
  53.5 99.7 all-reduce.7
  225.4 102.9 all-reduce.9
  330.5 29.0 all-gather.5
  371.0 99.7 all-reduce.11
  543.4 102.9 all-reduce.13
  648.6 29.0 all-gather.7
  689.1 99.7 all-reduce.15
  863.8 102.9 all-reduce.17
where the time goes:
time: 980 us; the launch traced here: 976 us
  waiting for transfers between devices  702 us (72%)
  other arithmetic  174 us (18%)
  matrix products  67 us (7%)
  between operations  18.5 us (2%)
  local copies, waits for them, and re-layouts  12.7 us (1%)
    psum x3, waiting for transfers between devices, project_scores(): lax.psum(partial_sum.astype(jnp.bfloat16), 'space').astype(jnp.float32)  309 us
    psum x3, waiting for transfers between devices, orthonormalize(): lax.psum(contract_rows(whole_basis, whole_basis).astype(jnp.bfloat16), 's...  299 us
    another operation x20, other arithmetic, orthonormalize(): lower_factor = jnp.linalg.cholesky(gram_sum / grid_total)  103 us
    all_gather x3, waiting for transfers between devices, widen_basis(): lax.all_gather(left_factor, 'col', axis=0, tiled=True)  92.8 us
    another operation x7, other arithmetic, orthonormalize(): jax.scipy.linalg.solve_triangular(lower_factor, identity_matrix, lower=True)  59.1 us
    dot_general x6, matrix products, contract_rows(): lax.dot_general(first, second, (((1,), (1,)), ((), ())), preferred_elemen...  32.3 us
    dot_general x3, matrix products, widen_basis(): jnp.dot(lax.all_gather(left_factor, 'col', axis=0, tiled=True), anomalies...  30.4 us
  transfers between devices with their start and end apart: 9, of which 9 were waited for; matrix products, arithmetic and copies ran while one was open for 0% of the time, Pallas kernels for 0%

commit v1 on v0

v1 whole, which is shorter than its diff:
```python
import jax
import jax.numpy as jnp
from jax import lax
from jax.experimental import pallas as pl
from jax.experimental.pallas import tpu as pltpu
from jax.sharding import PartitionSpec as P

f32, bf16 = jnp.float32, jnp.bfloat16
MESH = pl.DeviceIdType.MESH
PASSES = 3
ROWS, DAYS, POINTS = 256, 3712, 65536
LOCAL = 2048
OWN = 512
GROUP = 1280
PADDED = 3 * GROUP
PANEL = 32
CHUNKS = [(i * 512, 512) for i in range(7)] + [(3584, 128)]


def split3(a):
    first = a.astype(bf16)
    rest = a - first.astype(f32)
    second = rest.astype(bf16)
    return first, second, (rest - second.astype(f32)).astype(bf16)


def dot_split(a, b):
    a0, a1, a2 = split3(a)
    b0, b1, b2 = split3(b)
    left = jnp.concatenate([a0, a0, a1, a1, a0, a2], axis=1)
    right = jnp.concatenate([b0, b1, b0, b1, b2, b0], axis=0)
    return jnp.dot(left, right, preferred_element_type=f32)


def invert_panel(block):
    b = block.shape[0]
    tiles = b // 8
    sub = lax.broadcasted_iota(jnp.int32, (8, 128), 0)
    lane = lax.broadcasted_iota(jnp.int32, (8, 128), 1)
    cols = [
        [
            jnp.broadcast_to(block[8 * t : 8 * t + 8, c : c + 1], (8, 128)) if t >= c // 8 else None
            for t in range(tiles)
        ]
        for c in range(b)
    ]
    pivots = [None] * tiles

    def spread(v, i):
        return jnp.broadcast_to(v[i : i + 1, :], (8, 128))

    for j in range(b):
        tj, ij = j // 8, j % 8
        pivot = spread(cols[j][tj], ij)
        scale = 1.0 / pivot
        pivots[tj] = pivot if pivots[tj] is None else jnp.where(sub == ij, pivot, pivots[tj])
        col = cols[j]
        mult = [None] * tiles
        for t in range(tj, tiles):
            v = col[t] * scale
            mult[t] = jnp.where(sub > ij, v, 0.0) if t == tj else v
        for c in range(j + 1, b):
            a = spread(col[c // 8], c % 8)
            for t in range(c // 8, tiles):
                cols[c][t] = cols[c][t] - mult[t] * a
        for c in range(j):
            a = spread(cols[c][tj], ij)
            for t in range(tj, tiles):
                cols[c][t] = cols[c][t] - mult[t] * a
        cols[j] = [None] * tj + [
            (jnp.where(sub == ij, 1.0, -mult[t]) if t == tj else -mult[t]) for t in range(tj, tiles)
        ]
    out = []
    for t in range(tiles):
        acc = jnp.zeros((8, 128), f32)
        for c in range(8 * t + 8):
            acc = jnp.where(lane == c, cols[c][t], acc)
        acc = acc * lax.rsqrt(pivots[t])
        out.append(jnp.where(lane <= sub + 8 * t, acc, 0.0))
    return jnp.concatenate(out, axis=0)[:, :b]


def factor_step(t_ref, step):
    s, e = step * PANEL, (step + 1) * PANEL
    inv = invert_panel(t_ref[s:e, s:e])
    col = lax.broadcasted_iota(jnp.int32, (PANEL, ROWS), 1)
    row = lax.broadcasted_iota(jnp.int32, (PANEL, ROWS), 0)
    own = jnp.where((col >= s) & (col < e), jnp.where(col - s == row, 1.0, 0.0), t_ref[s:e, :])
    new = dot_split(inv, own)
    if e < ROWS:
        below = dot_split(t_ref[e:, s:e], inv.T)
        t_ref[e:, s:e] = jnp.zeros((ROWS - e, PANEL), f32)
        t_ref[e:, :] -= dot_split(below, new)
    t_ref[s:e, :] = jnp.where(col < e, new, 0.0)


def kernel(
    test_ref, a_hbm, eofs_ref, pcs_ref,
    a_ref, yacc, yown, basis, full, left, inv_ref, t_ref,
    wp, wc, ws, wf, r1, s2, r2, x3,
    gp, gc, g1, g2, g3, gf,
    a_sem, y_ss, y_rs, wc_ss, wc_rs, w_ss, w_rs, gc_ss, gc_rs, g_ss, g_rs,
):
    space, y = lax.axis_index("space"), lax.axis_index("col")
    at = (space // 8, y, (space // 2) % 4)
    core = space % 2

    def peer(axis, d):
        x, yy, z = (((at[i] + d) % 4) if i == axis else at[i] for i in range(3))
        return ((x * 4 + z) * 2 + core, yy)

    sibling = (space + 1 - 2 * core, y)

    def send(src, dst, ss, rs, device):
        copy = pltpu.make_async_remote_copy(
            src_ref=src, dst_ref=dst, send_sem=ss, recv_sem=rs, device_id=device, device_id_type=MESH
        )
        copy.start()
        return copy

    loads = []
    for i, (s, n) in enumerate(CHUNKS):
        copy = pltpu.make_async_copy(a_hbm.at[s : s + n, :], a_ref.at[s : s + n, :], a_sem.at[i])
        copy.start()
        loads.append(copy)

    barrier = pltpu.get_barrier_semaphore()
    for axis in range(3):
        for d in (1, 2, 3):
            pl.semaphore_signal(barrier, inc=1, device_id=peer(axis, d), device_id_type=MESH)
    pl.semaphore_signal(barrier, inc=1, device_id=sibling, device_id_type=MESH)

    wp[:, DAYS:] = jnp.zeros((ROWS, PADDED - DAYS), bf16)
    for i, (s, n) in enumerate(CHUNKS):
        loads[i].wait()
        part = jnp.dot(test_ref[:, s : s + n], a_ref[s : s + n, :], preferred_element_type=f32)
        if i == 0:
            yacc[...] = part
        elif i < len(CHUNKS) - 1:
            yacc[...] += part
        else:
            yown[...] = (yacc[...] + part).astype(bf16)

    pl.semaphore_wait(barrier, 10)

    my_rows = pl.ds(pl.multiple_of(64 * y, 64), 64)
    copies = []
    for d in (1, 2, 3):
        there = pl.ds(pl.multiple_of(OWN * ((y + d) % 4), OWN), OWN)
        copies.append(send(yown.at[:, there], basis.at[my_rows, :], y_ss.at[d - 1], y_rs.at[d - 1], peer(1, d)))
    own_points = pl.ds(pl.multiple_of(OWN * y, OWN), OWN)
    basis[my_rows, :] = yown[:, own_points]
    for copy in copies:
        copy.wait()

    half = pl.ds(pl.multiple_of(128 * core, 128), 128)
    other = pl.ds(pl.multiple_of(128 * (1 - core), 128), 128)
    g_own = pl.multiple_of(192 * core, 64)
    g_other = pl.multiple_of(192 * (1 - core), 64)

    def order(g):
        return g, (g + 1) % 3, (g + 2) % 3

    def full_block(i):
        full[:, i * OWN : (i + 1) * OWN] = jnp.dot(
            left[...], a_ref[:, i * OWN : (i + 1) * OWN], preferred_element_type=f32
        ).astype(bf16)

    def one_pass(k, carry):
        sent = []
        last = k == PASSES - 1

        gram = lax.dot_general(basis[...], basis[...], (((1,), (1,)), ((), ())), preferred_element_type=f32)
        gp[:ROWS, :] = gram[:, :128]
        gp[ROWS:, :] = gram[128:, 128:]
        g_core = send(gp.at[pl.ds(g_other, 192), :], gc, gc_ss.at[0], gc_rs.at[0], sibling)
        sent.append(g_core)

        w_core = []
        for g in range(3):
            s = GROUP * g
            n = min(GROUP, DAYS - s)
            wp[:, s : s + n] = lax.dot_general(
                basis[...], a_ref[s : s + n, own_points], (((1,), (1,)), ((), ())), preferred_element_type=f32
            ).astype(bf16)
            w_core.append(
                send(wp.at[other, s : s + GROUP], wc.at[:, s : s + GROUP], wc_ss.at[0, g], wc_rs.at[0, g], sibling)
            )
        sent += w_core

        def gram_send(stage, buf, g, value):
            axis = order(g)[stage]
            me = at[axis]
            buf[g, me] = value
            out = [
                send(buf.at[g, me], buf.at[g, me], g_ss.at[stage, g, d - 1], g_rs.at[stage, g, d - 1], peer(axis, d))
                for d in (1, 2, 3)
            ]
            sent.extend(out)
            return out

        def gram_sum(copies, buf, g):
            for copy in copies:
                copy.wait_recv()
            return (buf[g, 0] + buf[g, 1]) + (buf[g, 2] + buf[g, 3])

        g_core.wait_recv()
        gs1 = [
            gram_send(0, g1, g, gp[pl.ds(g_own + 64 * g, 64), :] + gc[64 * g : 64 * g + 64, :]) for g in range(3)
        ]

        ws1 = []
        for g in range(3):
            w_core[g].wait_recv()
            s = GROUP * g
            ws[:, s : s + GROUP] = (wp[half, s : s + GROUP].astype(f32) + wc[:, s : s + GROUP].astype(f32)).astype(bf16)
            axis = order(g)[0]
            for d in (1, 2, 3):
                rows = pl.ds(pl.multiple_of(32 * ((at[axis] + d) % 4), 32), 32)
                ws1.append(
                    send(
                        ws.at[rows, s : s + GROUP], r1.at[g, d - 1], w_ss.at[0, g, d - 1], w_rs.at[0, g, d - 1],
                        peer(axis, d),
                    )
                )
        sent += ws1

        pl.when(last)(lambda: full_block(0))

        gs2 = [gram_send(1, g2, g, gram_sum(gs1[g], g1, g)) for g in range(3)]

        ws2 = []
        for g in range(3):
            for copy in ws1[3 * g : 3 * g + 3]:
                copy.wait_recv()
            s = GROUP * g
            axis = order(g)[0]
            rows = pl.ds(pl.multiple_of(32 * at[axis], 32), 32)
            total = ws[rows, s : s + GROUP].astype(f32)
            for d in range(3):
                total += r1[g, d].astype(f32)
            s2[g] = total.astype(bf16)
            axis = order(g)[1]
            for d in (1, 2, 3):
                q = (at[axis] + d) % 4
                piece = s2.at[
                    g, pl.ds(pl.multiple_of(16 * (q // 2), 16), 16), pl.ds(pl.multiple_of(640 * (q % 2), 128), 640)
                ]
                ws2.append(send(piece, r2.at[g, d - 1], w_ss.at[1, g, d - 1], w_rs.at[1, g, d - 1], peer(axis, d)))
        sent += ws2

        pl.when(last)(lambda: full_block(1))

        gs3 = [gram_send(2, g3, g, gram_sum(gs2[g], g2, g)) for g in range(3)]

        ws3 = []
        for g in range(3):
            for copy in ws2[3 * g : 3 * g + 3]:
                copy.wait_recv()
            q = at[order(g)[1]]
            total = s2[
                g, pl.ds(pl.multiple_of(16 * (q // 2), 16), 16), pl.ds(pl.multiple_of(640 * (q % 2), 128), 640)
            ].astype(f32)
            for d in range(3):
                total += r2[g, d].astype(f32)
            axis = order(g)[2]
            me = at[axis]
            x3[g, me] = total.astype(bf16)
            for d in (1, 2, 3):
                ws3.append(
                    send(
                        x3.at[g, me], x3.at[g, me], w_ss.at[2, g, d - 1], w_rs.at[2, g, d - 1], peer(axis, d)
                    )
                )
        sent += ws3

        pl.when(last)(lambda: full_block(2))

        for g in range(3):
            gf[pl.ds(g_own + 64 * g, 64), :] = gram_sum(gs3[g], g3, g)
        g_back = send(
            gf.at[pl.ds(g_own, 192), :], gf.at[pl.ds(g_own, 192), :], gc_ss.at[1], gc_rs.at[1], sibling
        )
        sent.append(g_back)

        def spread_piece(g, quarter):
            first, second, _ = order(g)
            row, day = 128 * core + 32 * at[first], GROUP * g
            if quarter:
                return wf.at[pl.ds(pl.multiple_of(row, 32), 32), day : day + GROUP]
            q = at[second]
            return wf.at[
                pl.ds(pl.multiple_of(row + 16 * (q // 2), 16), 16),
                pl.ds(pl.multiple_of(day + 640 * (q % 2), 128), 640),
            ]

        ws4 = []
        for g in range(3):
            for copy in ws3[3 * g : 3 * g + 3]:
                copy.wait_recv()
            parts = [x3[g, i].astype(f32) for i in range(4)]
            piece = spread_piece(g, False)
            piece[...] = ((parts[0] + parts[1]) + (parts[2] + parts[3])).astype(bf16)
            axis = order(g)[1]
            for d in (1, 2, 3):
                ws4.append(send(piece, piece, w_ss.at[3, g, d - 1], w_rs.at[3, g, d - 1], peer(axis, d)))
        sent += ws4

        pl.when(last)(lambda: full_block(3))

        g_back.wait_recv()
        scale = 1.0 / POINTS
        t_ref[:, :128] = gf[:ROWS, :] * scale
        t_ref[128:, 128:] = gf[ROWS:, :] * scale
        t_ref[:128, 128:] = gf[128:ROWS, :].T * scale

        steps = ROWS // PANEL
        for step in range(0, 2):
            factor_step(t_ref, step)

        ws5 = []
        for g in range(3):
            for copy in ws4[3 * g : 3 * g + 3]:
                copy.wait_recv()
            piece = spread_piece(g, True)
            axis = order(g)[0]
            for d in (1, 2, 3):
                ws5.append(send(piece, piece, w_ss.at[4, g, d - 1], w_rs.at[4, g, d - 1], peer(axis, d)))
        sent += ws5

        for step in range(2, 7):
            factor_step(t_ref, step)

        w_back = []
        for g in range(3):
            for copy in ws5[3 * g : 3 * g + 3]:
                copy.wait_recv()
            s = GROUP * g
            w_back.append(
                send(wf.at[half, s : s + GROUP], wf.at[half, s : s + GROUP], wc_ss.at[1, g], wc_rs.at[1, g], sibling)
            )
        sent += w_back

        for step in range(7, steps):
            factor_step(t_ref, step)
        inv_ref[...] = t_ref[...].astype(bf16)

        for copy in w_back:
            copy.wait_recv()

        @pl.when(jnp.logical_not(last))
        def _():
            left[...] = (jnp.dot(inv_ref[...], wf[:, :DAYS], preferred_element_type=f32) * scale).astype(bf16)
            basis[...] = jnp.dot(left[...], a_ref[:, own_points], preferred_element_type=f32).astype(bf16)

        for copy in sent:
            copy.wait_send()
        return carry

    lax.fori_loop(0, PASSES, one_pass, 0)

    own_inverse = inv_ref[my_rows, :]
    eofs_ref[...] = jnp.dot(own_inverse, full[...], preferred_element_type=f32)
    pcs_ref[...] = jnp.dot(own_inverse, wf[:, :DAYS], preferred_element_type=f32) * (1.0 / POINTS)


def body(test_matrix, anomalies):
    vmem = pl.BlockSpec(memory_space=pltpu.VMEM)
    dma = pltpu.SemaphoreType.DMA
    return pl.pallas_call(
        kernel,
        out_shape=(jax.ShapeDtypeStruct((64, LOCAL), f32), jax.ShapeDtypeStruct((64, DAYS), f32)),
        in_specs=[vmem, pl.BlockSpec(memory_space=pl.ANY)],
        out_specs=(vmem, vmem),
        scratch_shapes=[
            pltpu.VMEM((DAYS, LOCAL), bf16),
            pltpu.VMEM((64, LOCAL), f32),
            pltpu.VMEM((64, LOCAL), bf16),
            pltpu.VMEM((ROWS, OWN), bf16),
            pltpu.VMEM((ROWS, LOCAL), bf16),
            pltpu.VMEM((ROWS, DAYS), bf16),
            pltpu.VMEM((ROWS, ROWS), bf16),
            pltpu.VMEM((ROWS, ROWS), f32),
            pltpu.VMEM((ROWS, PADDED), bf16),
            pltpu.VMEM((128, PADDED), bf16),
            pltpu.VMEM((128, PADDED), bf16),
            pltpu.VMEM((ROWS, PADDED), bf16),
            pltpu.VMEM((3, 3, 32, GROUP), bf16),
            pltpu.VMEM((3, 32, GROUP), bf16),
            pltpu.VMEM((3, 3, 16, 640), bf16),
            pltpu.VMEM((3, 4, 16, 640), bf16),
            pltpu.VMEM((384, 128), f32),
            pltpu.VMEM((192, 128), f32),
            pltpu.VMEM((3, 4, 64, 128), f32),
            pltpu.VMEM((3, 4, 64, 128), f32),
            pltpu.VMEM((3, 4, 64, 128), f32),
            pltpu.VMEM((384, 128), f32),
            dma((len(CHUNKS),)),
            dma((3,)),
            dma((3,)),
            dma((2, 3)),
            dma((2, 3)),
            dma((5, 3, 3)),
            dma((5, 3, 3)),
            dma((2,)),
            dma((2,)),
            dma((3, 3, 3)),
            dma((3, 3, 3)),
        ],
        compiler_params=pltpu.CompilerParams(collective_id=0, has_side_effects=True, vmem_limit_bytes=52 << 20),
        cost_estimate=pl.CostEstimate(flops=20 * 10**9, bytes_accessed=16 * 10**6, transcendentals=0),
        name="subspace_iteration",
    )(test_matrix, anomalies)


def solution(mesh):
    return jax.shard_map(
        body,
        mesh=mesh,
        in_specs=(P("col", None), P(None, "space")),
        out_specs=(P("col", "space"), P("col", None)),
        check_vma=False,
    )
```

time: 980 us -> 121 us (0.12)
  waiting for transfers between devices: 702 us -> 0 us
  other arithmetic: 174 us -> 0 us
  Pallas kernels: 0 us -> 117 us
  matrix products: 67 us -> 0 us
  between operations: 18.5 us -> 0.65 us
  local copies, waits for them, and re-layouts: 12.7 us -> 2.75 us
    psum x6 -> x0, waiting for transfers between devices: 608 us -> none  [the longest x3 309 us: project_scores(): lax.psum(partial_sum.astype(jnp.bfloat16), 'space').astype(jnp.float32)]
    another operation x27 -> x0, other arithmetic: 162 us -> none  [the longest x20 103 us: orthonormalize(): lower_factor = jnp.linalg.cholesky(gram_sum / grid_total)]
    pallas_call x0 -> x1, Pallas kernels: none -> 117 us  [body(): pl.pallas_call(kernel, out_shape=(jax.ShapeDtypeStruct((64, LOCAL), f32),...]
    all_gather x3 -> x0, waiting for transfers between devices: 92.8 us -> none  [widen_basis(): lax.all_gather(left_factor, 'col', axis=0, tiled=True)]
    dot_general x10 -> x0, matrix products: 63 us -> none  [the longest x6 32.3 us: contract_rows(): lax.dot_general(first, second, (((1,), (1,)), ((), ())), preferred_elemen...]
    another operation x28 -> x0, local copies, waits for them, and re-layouts: 12.3 us -> none  [the longest x22 12.3 us: orthonormalize(): jax.scipy.linalg.solve_triangular(lower_factor, identity_matrix, lower=True)]
  transfers between devices with their start and end apart: 9 -> 0, of which waited for: 9 -> 0; matrix products, arithmetic and copies ran while one was open for 0% -> 0% of each run, Pallas kernels for 0% -> 0%
where the time goes in v1:
time: 121 us; the launch traced here: 120 us
  Pallas kernels  117 us (97%)
  local copies, waits for them, and re-layouts  2.75 us (2%)
    pallas_call x1, Pallas kernels, body(): pl.pallas_call(kernel, out_shape=(jax.ShapeDtypeStruct((64, LOCAL), f32),...  117 us
    unnamed x4, local copies, waits for them, and re-layouts  2.75 us

profile of v1, /device:TPU:1, one launch (start us, length us, event | category | flops | bytes accessed | tf_op | source)
XLA Modules:
  0.0 120.4 jit_solution(14345066518688328963)
XLA Ops:
  0.6 0.0 copy-start
  0.6 1.0 copy-done
  1.7 117.0 %subspace_iteration.1 = (f32[64,2048]{1,0:T(8,128)S(1)}, f32[64,3712]{1,0:T(8,128)S(1)}) custom-call(bf16[64,3712]{1,0:T(8,128)(2,1)S(1)} %copy-done, bf16[3712,2048]{1,0:T(8,128)(2,1)} %a_hbm.1), custom_call_target="tpu_custom_call" | custom-call | flops 20000000000 | bytes 16000000 | tf_op jit(solution)/shard_map/subspace_iteration/pallas_call | solution.py:370
  118.7 0.8 copy.6
  119.5 0.9 copy.7
Async XLA Ops:
  0.6 1.0 copy-start

commit v2 on v0

v2 whole, which is shorter than its diff:
```python
import jax
import jax.numpy as jnp
from jax import lax
from jax.experimental import pallas as pl
from jax.experimental.pallas import tpu as pltpu
from jax.sharding import PartitionSpec as P

f32, bf16 = jnp.float32, jnp.bfloat16
MESH = pl.DeviceIdType.MESH
PASSES = 3
ROWS, DAYS, POINTS = 256, 3712, 65536
LOCAL = 2048
OWN = 512
WIDTHS = [384] * 5 + [256] * 7
UNITS, WIDEST = len(WIDTHS), max(WIDTHS)
STARTS = [sum(WIDTHS[:u]) for u in range(UNITS + 1)]
BATCHES = (0, 6, UNITS)
PANEL, STRIP = 32, 16
FAR_FIRST = (2, 1, 3)
SCHEDULE = (("factor", 4), ("share", 0), ("share", 1), ("factor", 2), ("use", 0), ("factor", 1), ("use", 1), ("factor", 1))


def split3(a):
    first = a.astype(bf16)
    rest = a - first.astype(f32)
    second = rest.astype(bf16)
    return first, second, (rest - second.astype(f32)).astype(bf16)


def eliminate_panel(tiles, s):
    count = len(tiles)
    sub = lax.broadcasted_iota(jnp.int32, (8, 128), 0)
    sub_all = lax.broadcasted_iota(jnp.int32, (8, ROWS), 0)
    lane_all = lax.broadcasted_iota(jnp.int32, (8, ROWS), 1)
    rows = list(tiles)
    square, shift = [None] * count, [None] * count

    def spread(v, i):
        return jnp.broadcast_to(v[i : i + 1, :], v.shape)

    def wide(v):
        return jnp.concatenate([v, v], axis=1)

    for c0 in range(0, 8 * count, STRIP):
        q0, q1 = c0 // 8, (c0 + STRIP) // 8
        cols = [
            {
                t: jnp.broadcast_to(rows[t][:, s + c0 + c : s + c0 + c + 1], (8, 128))
                for t in range(q0 + c // 8, count)
            }
            for c in range(STRIP)
        ]
        inside = (lane_all >= s + c0) & (lane_all < s + c0 + STRIP)
        for t in range(count):
            unit = jnp.where(lane_all - s - 8 * t == sub_all, 1.0, 0.0) if q0 <= t < q1 else 0.0
            rows[t] = jnp.where(inside, unit, rows[t])
        for j in range(0, STRIP, 2):
            q, i = q0 + j // 8, j % 8
            x, y = cols[j], cols[j + 1]
            a, b, c = spread(x[q], i), spread(x[q], i + 1), spread(y[q], i + 1)
            over_a = 1.0 / a
            over_det = 1.0 / (a * c - b * b)
            an, bn, cn = a * over_det, b * over_det, c * over_det
            sq = jnp.where(sub == i, over_a, an)
            sh = jnp.where(sub == i + 1, -b * over_a, 0.0)
            square[q] = sq if i == 0 else jnp.where(sub >= i, sq, square[q])
            shift[q] = sh if i == 0 else jnp.where(sub >= i, sh, shift[q])
            first, second = spread(rows[q], i), spread(rows[q], i + 1)
            for t in range(q, count):
                u = cn * x[t] - bn * y[t]
                v = an * y[t] - bn * x[t]
                if t == q:
                    u = jnp.where(sub > i + 1, u, 0.0)
                    v = jnp.where(sub > i + 1, v, 0.0)
                for k in range(j + 2, STRIP):
                    tk = q0 + k // 8
                    if t >= tk:
                        cols[k][t] = cols[k][t] - u * spread(x[tk], k % 8) - v * spread(y[tk], k % 8)
                if t > q or i < 6:
                    rows[t] = rows[t] - wide(u) * first - wide(v) * second
    out = []
    for t in range(count):
        down = jnp.concatenate([rows[t][7:8], rows[t][0:7]], axis=0)
        out.append((rows[t] + wide(shift[t]) * down) * wide(jnp.sqrt(square[t])))
    return jnp.concatenate(out, axis=0)


def factor_step(t_ref, step):
    s, e = step * PANEL, (step + 1) * PANEL
    new = eliminate_panel([t_ref[s + 8 * t : s + 8 * t + 8, :] for t in range(PANEL // 8)], s)
    if e < ROWS:
        n0, n1, n2 = split3(new)
        left = jnp.concatenate([n0, n0, n1, n1, n0, n2], axis=0)
        right = jnp.concatenate([n0, n1, n0, n1, n2, n0], axis=0)
        skip = e // 128 * 128
        update = lax.dot_general(left[:, skip:], right, (((0,), (0,)), ((), ())), preferred_element_type=f32)
        col = lax.broadcasted_iota(jnp.int32, (ROWS - e, ROWS), 1)
        t_ref[e:, :] = jnp.where((col >= s) & (col < e), 0.0, t_ref[e:, :]) - update[e - skip :]
    col = lax.broadcasted_iota(jnp.int32, (PANEL, ROWS), 1)
    t_ref[s:e, :] = jnp.where(col < e, new, 0.0)


def kernel(
    test_hbm, a_hbm, eofs_ref, pcs_ref,
    test_ref, a_ref, yown, yacc, basis, full, inv_ref, t_ref, norm_ref,
    wp, wc, ws, wf, r1, x2, x3,
    gp, gc, g1, g2, g3, gf,
    test_sem, a_sem, y_ss, y_rs, wc_ss, wc_rs, w_ss, w_rs, gc_ss, gc_rs, g_ss, g_rs,
):
    space, y = lax.axis_index("space"), lax.axis_index("col")
    at = (space // 8, y, (space // 2) % 4)
    core = space % 2

    def peer(axis, d):
        x, yy, z = (((at[i] + d) % 4) if i == axis else at[i] for i in range(3))
        return ((x * 4 + z) * 2 + core, yy)

    sibling = (space + 1 - 2 * core, y)

    def copy_to(device, src, dst, ss, rs):
        return pltpu.make_async_remote_copy(
            src_ref=src, dst_ref=dst, send_sem=ss, recv_sem=rs, device_id=device, device_id_type=MESH
        )

    def send(device, src, dst, ss, rs):
        copy = copy_to(device, src, dst, ss, rs)
        copy.start()
        return copy

    def points(i):
        return pl.ds(pl.multiple_of(OWN * i, OWN), OWN)

    load_test = pltpu.make_async_copy(test_hbm, test_ref, test_sem.at[0])
    load_test.start()
    blocks = [(y + d) % 4 for d in FAR_FIRST] + [y]
    loads = []
    for i, block in enumerate(blocks):
        for h in range(2):
            part = (pl.ds(h * (DAYS // 2), DAYS // 2), points(block))
            copy = pltpu.make_async_copy(a_hbm.at[part], a_ref.at[part], a_sem.at[i, h])
            copy.start()
            loads.append(copy)

    barrier = pltpu.get_barrier_semaphore()
    for axis in range(3):
        for d in FAR_FIRST:
            pl.semaphore_signal(barrier, inc=1, device_id=peer(axis, d), device_id_type=MESH)
    pl.semaphore_signal(barrier, inc=1, device_id=sibling, device_id_type=MESH)

    load_test.wait()

    my_rows = pl.ds(pl.multiple_of(64 * y, 64), 64)
    first_copies = []
    for i, block in enumerate(blocks):
        loads[2 * i].wait()
        loads[2 * i + 1].wait()
        product = jnp.dot(test_ref[...], a_ref[:, points(block)], preferred_element_type=f32).astype(bf16)
        if i == 0:
            pl.semaphore_wait(barrier, 10)
        if i < 3:
            yown[i] = product
            first_copies.append(
                send(peer(1, FAR_FIRST[i]), yown.at[i], basis.at[my_rows, :], y_ss.at[i], y_rs.at[i])
            )
        else:
            basis[my_rows, :] = product
    for copy in first_copies:
        copy.wait()

    half = pl.ds(pl.multiple_of(128 * core, 128), 128)
    other = pl.ds(pl.multiple_of(128 * (1 - core), 128), 128)
    g_own = pl.multiple_of(192 * core, 64)
    g_other = pl.multiple_of(192 * (1 - core), 64)

    def order(g):
        return g % 3, (g + 1) % 3, (g + 2) % 3

    def days(u):
        return slice(STARTS[u], STARTS[u + 1])

    def rows_of(i):
        return pl.ds(pl.multiple_of(32 * i, 32), 32)

    def one_pass(k, carry):
        last = k == PASSES - 1
        now, before = k % 2, (k + 1) % 2
        def send_three(axis, pair, ss, rs, three):
            for d in FAR_FIRST:
                src, dst = pair(d)
                send(peer(axis, d), src, dst, ss, rs)
            return copy_to(sibling, three, three, ss, rs)

        def full_block(i):
            product = jnp.dot(
                wf[before], a_ref[:, i * OWN : (i + 1) * OWN], preferred_element_type=f32
            ).astype(bf16)
            full[:, i * OWN : (i + 1) * OWN] = (
                jnp.dot(inv_ref[...], product, preferred_element_type=f32) * (1.0 / POINTS)
            ).astype(bf16)

        gram = lax.dot_general(basis[...], basis[...], (((1,), (1,)), ((), ())), preferred_element_type=f32)
        gp[:ROWS, :] = gram[:, :128]
        gp[ROWS:, :] = gram[128:, 128:]
        g_core = send(sibling, gp.at[pl.ds(g_other, 192), :], gc, gc_ss.at[0], gc_rs.at[0])

        w_core = []
        for u in range(UNITS):
            wp[:, days(u)] = lax.dot_general(
                basis[...], a_ref[days(u), points(y)], (((1,), (1,)), ((), ())), preferred_element_type=f32
            ).astype(bf16)
            w_core.append(send(sibling, wp.at[other, days(u)], wc.at[:, days(u)], wc_ss.at[0], wc_rs.at[0, u]))

        def gram_send(stage, buf, g, value):
            axis = order(g)[stage]
            mine = buf.at[g, at[axis]]
            mine[...] = value
            return send_three(axis, lambda d: (mine, mine), g_ss.at[stage], g_rs.at[stage, g], buf.at[g, 0:3])

        def gram_sum(arrived, buf, g):
            arrived.wait_recv()
            return (buf[g, 0] + buf[g, 1]) + (buf[g, 2] + buf[g, 3])

        def four(buf, u):
            parts = [buf[u, i, :, : WIDTHS[u]].astype(f32) for i in range(4)]
            return ((parts[0] + parts[1]) + (parts[2] + parts[3])).astype(bf16)

        g_core.wait_recv()
        gs1 = [
            gram_send(0, g1, g, gp[pl.ds(g_own + 64 * g, 64), :] + gc[64 * g : 64 * g + 64, :]) for g in range(3)
        ]

        def slots(buf, u):
            return buf.at[u, 0:3, :, : WIDTHS[u]]

        ws1 = []
        for u in range(UNITS):
            w_core[u].wait_recv()
            ws[:, days(u)] = (wp[half, days(u)].astype(f32) + wc[:, days(u)].astype(f32)).astype(bf16)
            axis = order(u)[0]
            ws1.append(
                send_three(
                    axis,
                    lambda d, u=u, axis=axis: (
                        ws.at[rows_of((at[axis] + d) % 4), days(u)], r1.at[u, d - 1, :, : WIDTHS[u]]
                    ),
                    w_ss.at[0], w_rs.at[0, u], slots(r1, u),
                )
            )

        pl.when(last)(lambda: full_block(0))

        gs2 = [gram_send(1, g2, g, gram_sum(gs1[g], g1, g)) for g in range(3)]

        ws2 = []
        for u in range(UNITS):
            ws1[u].wait_recv()
            first, axis, _ = order(u)
            total = ws[rows_of(at[first]), days(u)].astype(f32)
            for d in range(3):
                total += r1[u, d, :, : WIDTHS[u]].astype(f32)
            mine = x2.at[u, at[axis], :, : WIDTHS[u]]
            mine[...] = total.astype(bf16)
            ws2.append(send_three(axis, lambda d, m=mine: (m, m), w_ss.at[1], w_rs.at[1, u], slots(x2, u)))

        pl.when(last)(lambda: full_block(1))

        gs3 = [gram_send(2, g3, g, gram_sum(gs2[g], g2, g)) for g in range(3)]

        ws3 = []
        for u in range(UNITS):
            ws2[u].wait_recv()
            axis = order(u)[2]
            mine = x3.at[u, at[axis], :, : WIDTHS[u]]
            mine[...] = four(x2, u)
            ws3.append(send_three(axis, lambda d, m=mine: (m, m), w_ss.at[2], w_rs.at[2, u], slots(x3, u)))

        pl.when(last)(lambda: full_block(2))

        ws4, pieces = [], []

        def finish(u):
            ws3[u].wait_recv()
            piece = wf.at[now, rows_of(4 * core + at[order(u)[0]]), days(u)]
            piece[...] = four(x3, u)
            pieces.append(piece)

        def send_back(u):
            ws4.append(
                send_three(
                    order(u)[0], lambda d: (pieces[u], pieces[u]), w_ss.at[3], w_rs.at[3, u], slots(x3, u)
                )
            )

        for u in range(UNITS - 3):
            finish(u)
            send_back(u)
        for g in range(3):
            gf[pl.ds(g_own + 64 * g, 64), :] = gram_sum(gs3[g], g3, g)
        g_mine = gf.at[pl.ds(g_own, 192), :]
        g_back = send(sibling, g_mine, g_mine, gc_ss.at[1], gc_rs.at[1])
        for u in range(UNITS - 3, UNITS):
            finish(u)
        for u in range(UNITS - 3, UNITS):
            send_back(u)

        pl.when(last)(lambda: full_block(3))

        stage = wp.at[0:96, :]
        for i in range(3):
            copy_to(sibling, stage, stage, w_ss.at[i], w_rs.at[i, 0]).wait_send()
            copy_to(sibling, g1.at[:, 0:3], g1.at[:, 0:3], g_ss.at[i], g_rs.at[i, 0]).wait_send()
        copy_to(sibling, wc, wc, wc_ss.at[0], wc_rs.at[0, 0]).wait_send()
        g_core.wait_send()

        g_back.wait_recv()
        t_ref[:, :128] = gf[:ROWS, :]
        t_ref[128:, 128:] = gf[ROWS:, :]
        t_ref[:128, 128:] = gf[128:ROWS, :].T
        gram = t_ref[...]
        diagonal = jnp.where(
            lax.broadcasted_iota(jnp.int32, (ROWS, ROWS), 0) == lax.broadcasted_iota(jnp.int32, (ROWS, ROWS), 1), gram, 0.0
        )
        across = lax.rsqrt(jnp.sum(diagonal, axis=0, keepdims=True))
        down = lax.rsqrt(jnp.sum(diagonal, axis=1, keepdims=True))
        t_ref[...] = gram * down * across
        norm_ref[...] = across * POINTS**0.5

        w_back = []
        step = 0
        for what, n in SCHEDULE:
            if what == "factor":
                for _ in range(n):
                    factor_step(t_ref, step)
                    step += 1
            elif what == "share":
                for u in range(BATCHES[n], BATCHES[n + 1]):
                    ws4[u].wait_recv()
                    mine = wf.at[now, half, days(u)]
                    w_back.append(send(sibling, mine, mine, wc_ss.at[1], wc_rs.at[1, u]))
            else:
                for u in range(BATCHES[n], BATCHES[n + 1]):
                    w_back[u].wait_recv()
                own = slice(STARTS[BATCHES[n]], STARTS[BATCHES[n + 1]])
                product = jnp.dot(wf[now, :, own], a_ref[own, points(y)], preferred_element_type=f32)
                yacc[...] = product if n == 0 else yacc[...] + product
        inverse = (t_ref[...] * norm_ref[...]).astype(bf16)
        inv_ref[...] = inverse
        basis[...] = (
            jnp.dot(inverse, yacc[...].astype(bf16), preferred_element_type=f32) * (1.0 / POINTS)
        ).astype(bf16)

        copy_to(sibling, stage, stage, w_ss.at[3], w_rs.at[3, 0]).wait_send()
        copy_to(sibling, wc, wc, wc_ss.at[1], wc_rs.at[1, 0]).wait_send()
        g_back.wait_send()
        return carry

    lax.fori_loop(0, PASSES, one_pass, 0)

    own_inverse = inv_ref[my_rows, :]
    eofs_ref[...] = jnp.dot(own_inverse, full[...], preferred_element_type=f32)
    pcs_ref[...] = jnp.dot(own_inverse, wf[(PASSES - 1) % 2, :, :], preferred_element_type=f32) * (1.0 / POINTS)


def body(test_matrix, anomalies):
    vmem = pl.BlockSpec(memory_space=pltpu.VMEM)
    hbm = pl.BlockSpec(memory_space=pl.ANY)
    dma = pltpu.SemaphoreType.DMA
    return pl.pallas_call(
        kernel,
        out_shape=(jax.ShapeDtypeStruct((64, LOCAL), f32), jax.ShapeDtypeStruct((64, DAYS), f32)),
        in_specs=[hbm, hbm],
        out_specs=(vmem, vmem),
        scratch_shapes=[
            pltpu.VMEM((64, DAYS), bf16),
            pltpu.VMEM((DAYS, LOCAL), bf16),
            pltpu.VMEM((3, 64, OWN), bf16),
            pltpu.VMEM((ROWS, OWN), f32),
            pltpu.VMEM((ROWS, OWN), bf16),
            pltpu.VMEM((ROWS, LOCAL), bf16),
            pltpu.VMEM((ROWS, ROWS), bf16),
            pltpu.VMEM((ROWS, ROWS), f32),
            pltpu.VMEM((1, ROWS), f32),
            pltpu.VMEM((ROWS, DAYS), bf16),
            pltpu.VMEM((128, DAYS), bf16),
            pltpu.VMEM((128, DAYS), bf16),
            pltpu.VMEM((2, ROWS, DAYS), bf16),
            pltpu.VMEM((UNITS, 3, 32, WIDEST), bf16),
            pltpu.VMEM((UNITS, 4, 32, WIDEST), bf16),
            pltpu.VMEM((UNITS, 4, 32, WIDEST), bf16),
            pltpu.VMEM((384, 128), f32),
            pltpu.VMEM((192, 128), f32),
            pltpu.VMEM((3, 4, 64, 128), f32),
            pltpu.VMEM((3, 4, 64, 128), f32),
            pltpu.VMEM((3, 4, 64, 128), f32),
            pltpu.VMEM((384, 128), f32),
            dma((1,)),
            dma((4, 2)),
            dma((3,)),
            dma((3,)),
            dma((2,)),
            dma((2, UNITS)),
            dma((4,)),
            dma((4, UNITS)),
            dma((2,)),
            dma((2,)),
            dma((3,)),
            dma((3, 3)),
        ],
        compiler_params=pltpu.CompilerParams(collective_id=0, has_side_effects=True, vmem_limit_bytes=52 << 20),
        cost_estimate=pl.CostEstimate(flops=20 * 10**9, bytes_accessed=16 * 10**6, transcendentals=0),
        name="subspace_iteration",
    )(test_matrix, anomalies)


def solution(mesh):
    return jax.shard_map(
        body,
        mesh=mesh,
        in_specs=(P("col", None), P(None, "space")),
        out_specs=(P("col", "space"), P("col", None)),
        check_vma=False,
    )
```

time: 980 us -> 108 us (0.11)
  waiting for transfers between devices: 702 us -> 0 us
  other arithmetic: 174 us -> 0 us
  Pallas kernels: 0 us -> 105 us
  matrix products: 67 us -> 0 us
  between operations: 18.5 us -> 0.65 us
  local copies, waits for them, and re-layouts: 12.7 us -> 2.75 us
    psum x6 -> x0, waiting for transfers between devices: 608 us -> none  [the longest x3 309 us: project_scores(): lax.psum(partial_sum.astype(jnp.bfloat16), 'space').astype(jnp.float32)]
    another operation x27 -> x0, other arithmetic: 162 us -> none  [the longest x20 103 us: orthonormalize(): lower_factor = jnp.linalg.cholesky(gram_sum / grid_total)]
    pallas_call x0 -> x1, Pallas kernels: none -> 105 us  [body(): pl.pallas_call(kernel, out_shape=(jax.ShapeDtypeStruct((64, LOCAL), f32),...]
    all_gather x3 -> x0, waiting for transfers between devices: 92.8 us -> none  [widen_basis(): lax.all_gather(left_factor, 'col', axis=0, tiled=True)]
    dot_general x10 -> x0, matrix products: 63 us -> none  [the longest x6 32.3 us: contract_rows(): lax.dot_general(first, second, (((1,), (1,)), ((), ())), preferred_elemen...]
    another operation x28 -> x0, local copies, waits for them, and re-layouts: 12.3 us -> none  [the longest x22 12.3 us: orthonormalize(): jax.scipy.linalg.solve_triangular(lower_factor, identity_matrix, lower=True)]
  transfers between devices with their start and end apart: 9 -> 0, of which waited for: 9 -> 0; matrix products, arithmetic and copies ran while one was open for 0% -> 0% of each run, Pallas kernels for 0% -> 0%
where the time goes in v2:
time: 108 us
  Pallas kernels  105 us (97%)
  local copies, waits for them, and re-layouts  2.75 us (3%)
    pallas_call x1, Pallas kernels, body(): pl.pallas_call(kernel, out_shape=(jax.ShapeDtypeStruct((64, LOCAL), f32),...  105 us
    unnamed x4, local copies, waits for them, and re-layouts  2.75 us

profile of v2, /device:TPU:1, one launch (start us, length us, event | category | flops | bytes accessed | tf_op | source)
XLA Modules:
  0.0 108.0 jit_solution(12887272469125933251)
XLA Ops:
  0.6 0.0 copy-start
  0.6 1.0 copy-done
  1.7 104.6 %subspace_iteration.1 = (f32[64,2048]{1,0:T(8,128)S(1)}, f32[64,3712]{1,0:T(8,128)S(1)}) custom-call(bf16[64,3712]{1,0:T(8,128)(2,1)S(1)} %copy-done, bf16[3712,2048]{1,0:T(8,128)(2,1)} %a_hbm.1), custom_call_target="tpu_custom_call" | custom-call | flops 20000000000 | bytes 16000000 | tf_op jit(solution)/shard_map/subspace_iteration/pallas_call | solution.py:368
  106.2 0.8 copy.6
  107.0 0.9 copy.7
Async XLA Ops:
  0.6 1.0 copy-start

commit v3 on v2

--- a/solution.py
+++ b/solution.py
@@ -14,10 +14,11 @@
 WIDTHS = [384] * 5 + [256] * 7
 UNITS, WIDEST = len(WIDTHS), max(WIDTHS)
 STARTS = [sum(WIDTHS[:u]) for u in range(UNITS + 1)]
-BATCHES = (0, 6, UNITS)
+BATCHES = (0, 6, 10, UNITS)
+AHEAD = 6
 PANEL, STRIP = 32, 16
 FAR_FIRST = (2, 1, 3)
-SCHEDULE = (("factor", 4), ("share", 0), ("share", 1), ("factor", 2), ("use", 0), ("factor", 1), ("use", 1), ("factor", 1))
+SCHEDULE = (("factor", 4), ("share", 0), ("share", 1), ("share", 2), ("factor", 2), ("use", 0), ("factor", 1), ("use", 1), ("use", 2), ("factor", 1))
 
 
 def split3(a):
@@ -104,16 +105,16 @@
     test_hbm, a_hbm, eofs_ref, pcs_ref,
     test_ref, a_ref, yown, yacc, basis, full, inv_ref, t_ref, norm_ref,
     wp, wc, ws, wf, r1, x2, x3,
-    gp, gc, g1, g2, g3, gf,
+    gp, g1, g2, g3, gf,
     test_sem, a_sem, y_ss, y_rs, wc_ss, wc_rs, w_ss, w_rs, gc_ss, gc_rs, g_ss, g_rs,
 ):
     space, y = lax.axis_index("space"), lax.axis_index("col")
     at = (space // 8, y, (space // 2) % 4)
     core = space % 2
 
-    def peer(axis, d):
+    def peer(axis, d, across=0):
         x, yy, z = (((at[i] + d) % 4) if i == axis else at[i] for i in range(3))
-        return ((x * 4 + z) * 2 + core, yy)
+        return ((x * 4 + z) * 2 + (core + across) % 2, yy)
 
     sibling = (space + 1 - 2 * core, y)
 
@@ -144,7 +145,8 @@
     barrier = pltpu.get_barrier_semaphore()
     for axis in range(3):
         for d in FAR_FIRST:
-            pl.semaphore_signal(barrier, inc=1, device_id=peer(axis, d), device_id_type=MESH)
+            for across in (0, 1):
+                pl.semaphore_signal(barrier, inc=1, device_id=peer(axis, d, across), device_id_type=MESH)
     pl.semaphore_signal(barrier, inc=1, device_id=sibling, device_id_type=MESH)
 
     load_test.wait()
@@ -156,7 +158,7 @@
         loads[2 * i + 1].wait()
         product = jnp.dot(test_ref[...], a_ref[:, points(block)], preferred_element_type=f32).astype(bf16)
         if i == 0:
-            pl.semaphore_wait(barrier, 10)
+            pl.semaphore_wait(barrier, 19)
         if i < 3:
             yown[i] = product
             first_copies.append(
@@ -199,12 +201,12 @@
             ).astype(bf16)
 
         gram = lax.dot_general(basis[...], basis[...], (((1,), (1,)), ((), ())), preferred_element_type=f32)
-        gp[:ROWS, :] = gram[:, :128]
-        gp[ROWS:, :] = gram[128:, 128:]
-        g_core = send(sibling, gp.at[pl.ds(g_other, 192), :], gc, gc_ss.at[0], gc_rs.at[0])
+        gp[:ROWS, :] = gram[:, :128].astype(bf16)
+        gp[ROWS:, :] = gram[128:, 128:].astype(bf16)
 
         w_core = []
-        for u in range(UNITS):
+
+        def product_unit(u):
             wp[:, days(u)] = lax.dot_general(
                 basis[...], a_ref[days(u), points(y)], (((1,), (1,)), ((), ())), preferred_element_type=f32
             ).astype(bf16)
@@ -213,43 +215,65 @@
         def gram_send(stage, buf, g, value):
             axis = order(g)[stage]
             mine = buf.at[g, at[axis]]
-            mine[...] = value
+            mine[...] = value.astype(bf16)
             return send_three(axis, lambda d: (mine, mine), g_ss.at[stage], g_rs.at[stage, g], buf.at[g, 0:3])
 
         def gram_sum(arrived, buf, g):
             arrived.wait_recv()
-            return (buf[g, 0] + buf[g, 1]) + (buf[g, 2] + buf[g, 3])
+            parts = [buf[g, i].astype(f32) for i in range(4)]
+            return (parts[0] + parts[1]) + (parts[2] + parts[3])
 
         def four(buf, u):
             parts = [buf[u, i, :, : WIDTHS[u]].astype(f32) for i in range(4)]
             return ((parts[0] + parts[1]) + (parts[2] + parts[3])).astype(bf16)
 
-        g_core.wait_recv()
-        gs1 = [
-            gram_send(0, g1, g, gp[pl.ds(g_own + 64 * g, 64), :] + gc[64 * g : 64 * g + 64, :]) for g in range(3)
-        ]
-
         def slots(buf, u):
             return buf.at[u, 0:3, :, : WIDTHS[u]]
 
         ws1 = []
-        for u in range(UNITS):
+
+        def scatter(u):
             w_core[u].wait_recv()
             ws[:, days(u)] = (wp[half, days(u)].astype(f32) + wc[:, days(u)].astype(f32)).astype(bf16)
             axis = order(u)[0]
             ws1.append(
                 send_three(
                     axis,
-                    lambda d, u=u, axis=axis: (
-                        ws.at[rows_of((at[axis] + d) % 4), days(u)], r1.at[u, d - 1, :, : WIDTHS[u]]
-                    ),
+                    lambda d: (ws.at[rows_of((at[axis] + d) % 4), days(u)], r1.at[u, d - 1, :, : WIDTHS[u]]),
                     w_ss.at[0], w_rs.at[0, u], slots(r1, u),
                 )
             )
 
-        pl.when(last)(lambda: full_block(0))
-
-        gs2 = [gram_send(1, g2, g, gram_sum(gs1[g], g1, g)) for g in range(3)]
+        gs1 = []
+        for g in range(3):
+            slot = 4 * core + at[g]
+            mine = gp.at[pl.ds(g_own + 64 * g, 64), :]
+            theirs = gp.at[pl.ds(g_other + 64 * g, 64), :]
+            for d in FAR_FIRST:
+                send(peer(g, d, 1), theirs, g1.at[g, slot], g_ss.at[0], g_rs.at[0, g])
+                send(peer(g, d), mine, g1.at[g, slot], g_ss.at[0], g_rs.at[0, g])
+            send(sibling, theirs, g1.at[g, slot], g_ss.at[0], g_rs.at[0, g])
+            g1[g, slot] = mine[...]
+            gs1.append(copy_to(sibling, g1.at[g, 0:7], g1.at[g, 0:7], g_ss.at[0], g_rs.at[0, g]))
+
+        for u in range(UNITS):
+            product_unit(u)
+            if u >= AHEAD:
+                scatter(u - AHEAD)
+        for u in range(UNITS - AHEAD, UNITS):
+            scatter(u)
+
+        @pl.when(last)
+        def _():
+            full_block(0)
+            full_block(1)
+
+        gs2 = []
+        for g in range(3):
+            gs1[g].wait_recv()
+            parts = [g1[g, i].astype(f32) for i in range(8)]
+            total = ((parts[0] + parts[1]) + (parts[2] + parts[3])) + ((parts[4] + parts[5]) + (parts[6] + parts[7]))
+            gs2.append(gram_send(1, g2, g, total))
 
         ws2 = []
         for u in range(UNITS):
@@ -262,7 +286,7 @@
             mine[...] = total.astype(bf16)
             ws2.append(send_three(axis, lambda d, m=mine: (m, m), w_ss.at[1], w_rs.at[1, u], slots(x2, u)))
 
-        pl.when(last)(lambda: full_block(1))
+        pl.when(last)(lambda: full_block(2))
 
         gs3 = [gram_send(2, g3, g, gram_sum(gs2[g], g2, g)) for g in range(3)]
 
@@ -274,7 +298,7 @@
             mine[...] = four(x2, u)
             ws3.append(send_three(axis, lambda d, m=mine: (m, m), w_ss.at[2], w_rs.at[2, u], slots(x3, u)))
 
-        pl.when(last)(lambda: full_block(2))
+        pl.when(last)(lambda: full_block(3))
 
         ws4, pieces = [], []
 
@@ -303,27 +327,26 @@
         for u in range(UNITS - 3, UNITS):
             send_back(u)
 
-        pl.when(last)(lambda: full_block(3))
-
         stage = wp.at[0:96, :]
         for i in range(3):
             copy_to(sibling, stage, stage, w_ss.at[i], w_rs.at[i, 0]).wait_send()
-            copy_to(sibling, g1.at[:, 0:3], g1.at[:, 0:3], g_ss.at[i], g_rs.at[i, 0]).wait_send()
+        for i, three in enumerate((g1.at[:, 0:7], g2.at[:, 0:3], g2.at[:, 0:3])):
+            copy_to(sibling, three, three, g_ss.at[i], g_rs.at[i, 0]).wait_send()
         copy_to(sibling, wc, wc, wc_ss.at[0], wc_rs.at[0, 0]).wait_send()
-        g_core.wait_send()
 
         g_back.wait_recv()
-        t_ref[:, :128] = gf[:ROWS, :]
-        t_ref[128:, 128:] = gf[ROWS:, :]
-        t_ref[:128, 128:] = gf[128:ROWS, :].T
-        gram = t_ref[...]
-        diagonal = jnp.where(
-            lax.broadcasted_iota(jnp.int32, (ROWS, ROWS), 0) == lax.broadcasted_iota(jnp.int32, (ROWS, ROWS), 1), gram, 0.0
-        )
-        across = lax.rsqrt(jnp.sum(diagonal, axis=0, keepdims=True))
-        down = lax.rsqrt(jnp.sum(diagonal, axis=1, keepdims=True))
-        t_ref[...] = gram * down * across
-        norm_ref[...] = across * POINTS**0.5
+        quarter = (128, 128)
+        on = lax.broadcasted_iota(jnp.int32, quarter, 0) == lax.broadcasted_iota(jnp.int32, quarter, 1)
+        upper, cross, lower = gf[:128, :], gf[128:ROWS, :], gf[ROWS:, :]
+        diagonal = [jnp.where(on, upper, 0.0), jnp.where(on, lower, 0.0)]
+        across = [lax.rsqrt(jnp.sum(v, axis=0, keepdims=True)) for v in diagonal]
+        down = [lax.rsqrt(jnp.sum(v, axis=1, keepdims=True)) for v in diagonal]
+        cross = cross * down[1] * across[0]
+        t_ref[:128, :128] = upper * down[0] * across[0]
+        t_ref[128:, 128:] = lower * down[1] * across[1]
+        t_ref[128:, :128] = cross
+        t_ref[:128, 128:] = cross.T
+        norm_ref[...] = jnp.concatenate(across, axis=1) * POINTS**0.5
 
         w_back = []
         step = 0
@@ -387,11 +410,10 @@
             pltpu.VMEM((UNITS, 3, 32, WIDEST), bf16),
             pltpu.VMEM((UNITS, 4, 32, WIDEST), bf16),
             pltpu.VMEM((UNITS, 4, 32, WIDEST), bf16),
-            pltpu.VMEM((384, 128), f32),
-            pltpu.VMEM((192, 128), f32),
-            pltpu.VMEM((3, 4, 64, 128), f32),
-            pltpu.VMEM((3, 4, 64, 128), f32),
-            pltpu.VMEM((3, 4, 64, 128), f32),
+            pltpu.VMEM((384, 128), bf16),
+            pltpu.VMEM((3, 8, 64, 128), bf16),
+            pltpu.VMEM((3, 4, 64, 128), bf16),
+            pltpu.VMEM((3, 4, 64, 128), bf16),
             pltpu.VMEM((384, 128), f32),
             dma((1,)),
             dma((4, 2)),

time: 108 us -> 99.1 us (0.918)
  Pallas kernels: 105 us -> 95.6 us
    pallas_call x1, Pallas kernels: 105 us -> 95.6 us  [body(): pl.pallas_call(kernel, out_shape=(jax.ShapeDtypeStruct((64, LOCAL), f32),...]
where the time goes in v3:
time: 99.1 us; the launch traced here: 99 us
  Pallas kernels  95.6 us (96%)
  local copies, waits for them, and re-layouts  2.75 us (3%)
    pallas_call x1, Pallas kernels, body(): pl.pallas_call(kernel, out_shape=(jax.ShapeDtypeStruct((64, LOCAL), f32),...  95.6 us
    unnamed x4, local copies, waits for them, and re-layouts  2.75 us

profile of v3, /device:TPU:1, one launch (start us, length us, event | category | flops | bytes accessed | tf_op | source)
XLA Modules:
  0.0 99.0 jit_solution(6737407799430130013)
XLA Ops:
  0.6 0.0 copy-start
  0.6 1.0 %copy-done = bf16[64,3712]{1,0:T(8,128)(2,1)S(1)} copy-done((bf16[64,3712]{1,0:T(8,128)(2,1)S(1)}, bf16[64,3712]{1,0:T(8,128)(2,1)}, u32[]{:S(2)}) %copy-start) | copy-done | bytes 475160
  1.7 95.6 %subspace_iteration.1 = (f32[64,2048]{1,0:T(8,128)S(1)}, f32[64,3712]{1,0:T(8,128)S(1)}) custom-call(bf16[64,3712]{1,0:T(8,128)(2,1)S(1)} %copy-done, bf16[3712,2048]{1,0:T(8,128)(2,1)} %a_hbm.1), custom_call_target="tpu_custom_call" | custom-call | flops 20000000000 | bytes 16000000 | tf_op jit(solution)/shard_map/subspace_iteration/pallas_call | solution.py:391
  97.2 0.8 copy.6
  98.0 0.9 copy.7
Async XLA Ops:
  0.6 1.0 %copy-start = (bf16[64,3712]{1,0:T(8,128)(2,1)S(1)}, bf16[64,3712]{1,0:T(8,128)(2,1)}, u32[]{:S(2)}) copy-start(bf16[64,3712]{1,0:T(8,128)(2,1)} %test_hbm.1) | copy-start | bytes 1425412

commit v4 on v3

--- a/solution.py
+++ b/solution.py
@@ -15,10 +15,25 @@
 UNITS, WIDEST = len(WIDTHS), max(WIDTHS)
 STARTS = [sum(WIDTHS[:u]) for u in range(UNITS + 1)]
 BATCHES = (0, 6, 10, UNITS)
-AHEAD = 6
+AHEAD = 4
 PANEL, STRIP = 32, 16
 FAR_FIRST = (2, 1, 3)
-SCHEDULE = (("factor", 4), ("share", 0), ("share", 1), ("share", 2), ("factor", 2), ("use", 0), ("factor", 1), ("use", 1), ("use", 2), ("factor", 1))
+SCHEDULE = (
+    ("gram", 0),
+    ("back", 9),
+    ("close", 0),
+    ("build", 0),
+    ("factor", 4),
+    ("share", 6),
+    ("share", 10),
+    ("share", 12),
+    ("factor", 2),
+    ("use", 0),
+    ("factor", 1),
+    ("use", 1),
+    ("use", 2),
+    ("factor", 1),
+)
 
 
 def split3(a):
@@ -192,13 +207,10 @@
                 send(peer(axis, d), src, dst, ss, rs)
             return copy_to(sibling, three, three, ss, rs)
 
-        def full_block(i):
-            product = jnp.dot(
-                wf[before], a_ref[:, i * OWN : (i + 1) * OWN], preferred_element_type=f32
-            ).astype(bf16)
-            full[:, i * OWN : (i + 1) * OWN] = (
-                jnp.dot(inv_ref[...], product, preferred_element_type=f32) * (1.0 / POINTS)
-            ).astype(bf16)
+        def full_block(d):
+            block = points((y + d) % 4)
+            product = jnp.dot(wf[before], a_ref[:, block], preferred_element_type=f32).astype(bf16)
+            full[:, block] = (jnp.dot(inv_ref[...], product, preferred_element_type=f32) * (1.0 / POINTS)).astype(bf16)
 
         gram = lax.dot_general(basis[...], basis[...], (((1,), (1,)), ((), ())), preferred_element_type=f32)
         gp[:ROWS, :] = gram[:, :128].astype(bf16)
@@ -263,10 +275,7 @@
         for u in range(UNITS - AHEAD, UNITS):
             scatter(u)
 
-        @pl.when(last)
-        def _():
-            full_block(0)
-            full_block(1)
+        pl.when(last)(lambda: full_block(1))
 
         gs2 = []
         for g in range(3):
@@ -298,7 +307,10 @@
             mine[...] = four(x2, u)
             ws3.append(send_three(axis, lambda d, m=mine: (m, m), w_ss.at[2], w_rs.at[2, u], slots(x3, u)))
 
-        pl.when(last)(lambda: full_block(3))
+        @pl.when(last)
+        def _():
+            full_block(3)
+            full[:, points(y)] = basis[...]
 
         ws4, pieces = [], []
 
@@ -315,17 +327,64 @@
                 )
             )
 
-        for u in range(UNITS - 3):
-            finish(u)
-            send_back(u)
-        for g in range(3):
-            gf[pl.ds(g_own + 64 * g, 64), :] = gram_sum(gs3[g], g3, g)
-        g_mine = gf.at[pl.ds(g_own, 192), :]
-        g_back = send(sibling, g_mine, g_mine, gc_ss.at[1], gc_rs.at[1])
-        for u in range(UNITS - 3, UNITS):
-            finish(u)
-        for u in range(UNITS - 3, UNITS):
-            send_back(u)
+        def gram_back():
+            for g in range(3):
+                gf[pl.ds(g_own + 64 * g, 64), :] = gram_sum(gs3[g], g3, g)
+            mine = gf.at[pl.ds(g_own, 192), :]
+            return send(sibling, mine, mine, gc_ss.at[1], gc_rs.at[1])
+
+        def build():
+            g_back.wait_recv()
+            quarter = (128, 128)
+            on = lax.broadcasted_iota(jnp.int32, quarter, 0) == lax.broadcasted_iota(jnp.int32, quarter, 1)
+            upper, cross, lower = gf[:128, :], gf[128:ROWS, :], gf[ROWS:, :]
+            diagonal = [jnp.where(on, upper, 0.0), jnp.where(on, lower, 0.0)]
+            across = [lax.rsqrt(jnp.sum(v, axis=0, keepdims=True)) for v in diagonal]
+            down = [lax.rsqrt(jnp.sum(v, axis=1, keepdims=True)) for v in diagonal]
+            cross = cross * down[1] * across[0]
+            t_ref[:128, :128] = upper * down[0] * across[0]
+            t_ref[128:, 128:] = lower * down[1] * across[1]
+            t_ref[128:, :128] = cross
+            t_ref[:128, 128:] = cross.T
+            norm_ref[...] = jnp.concatenate(across, axis=1) * POINTS**0.5
+
+        def share(u):
+            ws4[u].wait_recv()
+            mine = wf.at[now, half, days(u)]
+            return send(sibling, mine, mine, wc_ss.at[1], wc_rs.at[1, u])
+
+        def use(batch):
+            for u in range(BATCHES[batch], BATCHES[batch + 1]):
+                w_back[u].wait_recv()
+            own = slice(STARTS[BATCHES[batch]], STARTS[BATCHES[batch + 1]])
+            product = jnp.dot(wf[now, :, own], a_ref[own, points(y)], preferred_element_type=f32)
+            yacc[...] = product if batch == 0 else yacc[...] + product
+
+        w_back = []
+        step = 0
+        for what, n in SCHEDULE:
+            if what == "gram":
+                g_back = gram_back()
+            elif what == "back":
+                for u in range(len(pieces), n):
+                    finish(u)
+                    send_back(u)
+            elif what == "close":
+                for u in range(UNITS - 3, UNITS):
+                    finish(u)
+                for u in range(UNITS - 3, UNITS):
+                    send_back(u)
+            elif what == "build":
+                build()
+            elif what == "factor":
+                for _ in range(n):
+                    factor_step(t_ref, step)
+                    step += 1
+            elif what == "share":
+                for u in range(len(w_back), n):
+                    w_back.append(share(u))
+            else:
+                use(n)
 
         stage = wp.at[0:96, :]
         for i in range(3):
@@ -334,38 +393,6 @@
             copy_to(sibling, three, three, g_ss.at[i], g_rs.at[i, 0]).wait_send()
         copy_to(sibling, wc, wc, wc_ss.at[0], wc_rs.at[0, 0]).wait_send()
 
-        g_back.wait_recv()
-        quarter = (128, 128)
-        on = lax.broadcasted_iota(jnp.int32, quarter, 0) == lax.broadcasted_iota(jnp.int32, quarter, 1)
-        upper, cross, lower = gf[:128, :], gf[128:ROWS, :], gf[ROWS:, :]
-        diagonal = [jnp.where(on, upper, 0.0), jnp.where(on, lower, 0.0)]
-        across = [lax.rsqrt(jnp.sum(v, axis=0, keepdims=True)) for v in diagonal]
-        down = [lax.rsqrt(jnp.sum(v, axis=1, keepdims=True)) for v in diagonal]
-        cross = cross * down[1] * across[0]
-        t_ref[:128, :128] = upper * down[0] * across[0]
-        t_ref[128:, 128:] = lower * down[1] * across[1]
-        t_ref[128:, :128] = cross
-        t_ref[:128, 128:] = cross.T
-        norm_ref[...] = jnp.concatenate(across, axis=1) * POINTS**0.5
-
-        w_back = []
-        step = 0
-        for what, n in SCHEDULE:
-            if what == "factor":
-                for _ in range(n):
-                    factor_step(t_ref, step)
-                    step += 1
-            elif what == "share":
-                for u in range(BATCHES[n], BATCHES[n + 1]):
-                    ws4[u].wait_recv()
-                    mine = wf.at[now, half, days(u)]
-                    w_back.append(send(sibling, mine, mine, wc_ss.at[1], wc_rs.at[1, u]))
-            else:
-                for u in range(BATCHES[n], BATCHES[n + 1]):
-                    w_back[u].wait_recv()
-                own = slice(STARTS[BATCHES[n]], STARTS[BATCHES[n + 1]])
-                product = jnp.dot(wf[now, :, own], a_ref[own, points(y)], preferred_element_type=f32)
-                yacc[...] = product if n == 0 else yacc[...] + product
         inverse = (t_ref[...] * norm_ref[...]).astype(bf16)
         inv_ref[...] = inverse
         basis[...] = (

time: 99.1 us -> 96.8 us (0.977)
  Pallas kernels: 95.6 us -> 93.3 us
    pallas_call x1, Pallas kernels: 95.6 us -> 93.3 us  [body(): pl.pallas_call(kernel, out_shape=(jax.ShapeDtypeStruct((64, LOCAL), f32),...]
where the time goes in v4:
time: 96.8 us; the launch traced here: 96.7 us
  Pallas kernels  93.3 us (96%)
  local copies, waits for them, and re-layouts  2.75 us (3%)
    pallas_call x1, Pallas kernels, body(): pl.pallas_call(kernel, out_shape=(jax.ShapeDtypeStruct((64, LOCAL), f32),...  93.3 us
    unnamed x4, local copies, waits for them, and re-layouts  2.75 us

profile of v4, /device:TPU:1, one launch (start us, length us, event | category | flops | bytes accessed | tf_op | source)
XLA Modules:
  0.0 96.7 jit_solution(17368189830562335356)
XLA Ops:
  0.6 0.0 copy-start
  0.6 1.0 %copy-done = bf16[64,3712]{1,0:T(8,128)(2,1)S(1)} copy-done((bf16[64,3712]{1,0:T(8,128)(2,1)S(1)}, bf16[64,3712]{1,0:T(8,128)(2,1)}, u32[]{:S(2)}) %copy-start) | copy-done | bytes 475160
  1.7 93.3 %subspace_iteration.1 = (f32[64,2048]{1,0:T(8,128)S(1)}, f32[64,3712]{1,0:T(8,128)S(1)}) custom-call(bf16[64,3712]{1,0:T(8,128)(2,1)S(1)} %copy-done, bf16[3712,2048]{1,0:T(8,128)(2,1)} %a_hbm.1), custom_call_target="tpu_custom_call" | custom-call | flops 20000000000 | bytes 16000000 | tf_op jit(solution)/shard_map/subspace_iteration/pallas_call | solution.py:418
  95.0 0.8 copy.6
  95.8 0.9 copy.7
Async XLA Ops:
  0.6 1.0 %copy-start = (bf16[64,3712]{1,0:T(8,128)(2,1)S(1)}, bf16[64,3712]{1,0:T(8,128)(2,1)}, u32[]{:S(2)}) copy-start(bf16[64,3712]{1,0:T(8,128)(2,1)} %test_hbm.1) | copy-start | bytes 1425412

commit v5 on v4

--- a/solution.py
+++ b/solution.py
@@ -11,22 +11,22 @@
 ROWS, DAYS, POINTS = 256, 3712, 65536
 LOCAL = 2048
 OWN = 512
-WIDTHS = [384] * 5 + [256] * 7
+WIDTHS = [512] * 2 + [384] * 7
 UNITS, WIDEST = len(WIDTHS), max(WIDTHS)
 STARTS = [sum(WIDTHS[:u]) for u in range(UNITS + 1)]
-BATCHES = (0, 6, 10, UNITS)
+BATCHES = (0, 4, 7, UNITS)
 AHEAD = 4
 PANEL, STRIP = 32, 16
 FAR_FIRST = (2, 1, 3)
 SCHEDULE = (
     ("gram", 0),
-    ("back", 9),
+    ("back", 6),
     ("close", 0),
     ("build", 0),
     ("factor", 4),
-    ("share", 6),
-    ("share", 10),
-    ("share", 12),
+    ("share", 4),
+    ("share", 7),
+    ("share", 9),
     ("factor", 2),
     ("use", 0),
     ("factor", 1),

time: 96.8 us -> 95.4 us (0.986)
  Pallas kernels: 93.3 us -> 91.9 us
    pallas_call x1, Pallas kernels: 93.3 us -> 91.9 us  [body(): pl.pallas_call(kernel, out_shape=(jax.ShapeDtypeStruct((64, LOCAL), f32),...]
where the time goes in v5:
time: 95.4 us; the launch traced here: 95.3 us
  Pallas kernels  91.9 us (96%)
  local copies, waits for them, and re-layouts  2.75 us (3%)
    pallas_call x1, Pallas kernels, body(): pl.pallas_call(kernel, out_shape=(jax.ShapeDtypeStruct((64, LOCAL), f32),...  91.9 us
    unnamed x4, local copies, waits for them, and re-layouts  2.75 us

profile of v5, /device:TPU:1, one launch (start us, length us, event | category | flops | bytes accessed | tf_op | source)
XLA Modules:
  0.0 95.3 jit_solution(3814485954975649189)
XLA Ops:
  0.6 0.0 copy-start
  0.6 1.0 %copy-done = bf16[64,3712]{1,0:T(8,128)(2,1)S(1)} copy-done((bf16[64,3712]{1,0:T(8,128)(2,1)S(1)}, bf16[64,3712]{1,0:T(8,128)(2,1)}, u32[]{:S(2)}) %copy-start) | copy-done | bytes 475160
  1.7 91.9 %subspace_iteration.1 = (f32[64,2048]{1,0:T(8,128)S(1)}, f32[64,3712]{1,0:T(8,128)S(1)}) custom-call(bf16[64,3712]{1,0:T(8,128)(2,1)S(1)} %copy-done, bf16[3712,2048]{1,0:T(8,128)(2,1)} %a_hbm.1), custom_call_target="tpu_custom_call" | custom-call | flops 20000000000 | bytes 16000000 | tf_op jit(solution)/shard_map/subspace_iteration/pallas_call | solution.py:418
  93.5 0.8 copy.6
  94.3 0.9 copy.7
Async XLA Ops:
  0.6 1.0 %copy-start = (bf16[64,3712]{1,0:T(8,128)(2,1)S(1)}, bf16[64,3712]{1,0:T(8,128)(2,1)}, u32[]{:S(2)}) copy-start(bf16[64,3712]{1,0:T(8,128)(2,1)} %test_hbm.1) | copy-start | bytes 1425412

commit v6 on v5

--- a/solution.py
+++ b/solution.py
@@ -15,7 +15,7 @@
 UNITS, WIDEST = len(WIDTHS), max(WIDTHS)
 STARTS = [sum(WIDTHS[:u]) for u in range(UNITS + 1)]
 BATCHES = (0, 4, 7, UNITS)
-AHEAD = 4
+AHEAD = 3
 PANEL, STRIP = 32, 16
 FAR_FIRST = (2, 1, 3)
 SCHEDULE = (

time: 95.4 us -> 94.8 us (level)
  no operation moved by 1% of the time
where the time goes in v6:
time: 94.8 us; the launch traced here: 94.7 us
  Pallas kernels  91.3 us (96%)
  local copies, waits for them, and re-layouts  2.75 us (3%)
    pallas_call x1, Pallas kernels, body(): pl.pallas_call(kernel, out_shape=(jax.ShapeDtypeStruct((64, LOCAL), f32),...  91.3 us
    unnamed x4, local copies, waits for them, and re-layouts  2.75 us

profile of v6, /device:TPU:1, one launch (start us, length us, event | category | flops | bytes accessed | tf_op | source)
XLA Modules:
  0.0 94.7 jit_solution(12166847377571924886)
XLA Ops:
  0.6 0.0 copy-start
  0.6 1.0 %copy-done = bf16[64,3712]{1,0:T(8,128)(2,1)S(1)} copy-done((bf16[64,3712]{1,0:T(8,128)(2,1)S(1)}, bf16[64,3712]{1,0:T(8,128)(2,1)}, u32[]{:S(2)}) %copy-start) | copy-done | bytes 475160
  1.7 91.3 %subspace_iteration.1 = (f32[64,2048]{1,0:T(8,128)S(1)}, f32[64,3712]{1,0:T(8,128)S(1)}) custom-call(bf16[64,3712]{1,0:T(8,128)(2,1)S(1)} %copy-done, bf16[3712,2048]{1,0:T(8,128)(2,1)} %a_hbm.1), custom_call_target="tpu_custom_call" | custom-call | flops 20000000000 | bytes 16000000 | tf_op jit(solution)/shard_map/subspace_iteration/pallas_call | solution.py:418
  93.0 0.8 copy.6
  93.8 0.9 copy.7
Async XLA Ops:
  0.6 1.0 %copy-start = (bf16[64,3712]{1,0:T(8,128)(2,1)S(1)}, bf16[64,3712]{1,0:T(8,128)(2,1)}, u32[]{:S(2)}) copy-start(bf16[64,3712]{1,0:T(8,128)(2,1)} %test_hbm.1) | copy-start | bytes 1425412
